TPU v7x, 256 devices: a whole 4x4x8 slice. The times are simulated.
256 devices in a mesh: layer: 16 (over y_lo, x, core), query: 16 (over z, y_hi).
Axes of the slice: x: 4, y: 4 (y_hi: 2, y_lo: 2; y = y_hi * 2 + y_lo), z: 8, core: 2. Of those that a mesh axis runs over, the one named last changes fastest.
Arguments:
- queries: bfloat16 [16384, 16, 4096], P('query', 'layer'), may hold values from -6 to 6
- train_grads: bfloat16 [1024, 16, 4096], P('query', 'layer'), may hold values from -6 to 6
- basis_out: float32 [16, 64, 64], P('layer'), may hold values from -0.75 to 0.75
- basis_in: float32 [16, 64, 64], P('layer'), may hold values from -0.75 to 0.75
- eig_values: float32 [16, 4096], P('layer'), may hold values from 0.1 to 2
- train_order: int32 [1024], replicated, may hold values from 0 to 1023, each once
Outputs:
- scores: float32 [1024, 16384], P('layer', 'query')
Inputs may be any that keep to these rules, and one draw needn't show every extreme that they name: `train_order`: a permutation of the 1024 training examples.
All inputs are finite; a program needn't handle non-finite values.
Results may differ from a plain program's by a relative error of at most 0.0029.
Values may be sent and summed in bfloat16 or wider, within the bound.
No kernel may reach another device: no remote copies, remote signals or barrier semaphores. Data moves between devices by JAX's collectives and lax.ppermute only.
A program may use at most 64 MiB of HBM per device.

v0:
```python
import jax
import jax.numpy as jnp
from jax import lax
from jax.sharding import PartitionSpec as P


def per_device(queries, train_grads, basis_out, basis_in, eig_values, train_order):
    query_rows, local_layers, feat_size = queries.shape
    train_rows = train_grads.shape[0]
    side = basis_out.shape[1]
    grads_full = train_grads.astype(jnp.float32).reshape(train_rows, local_layers, side, side)
    rotated = jnp.einsum(
        "lab,elac,lcd->elbd", basis_out, grads_full, basis_in, precision=lax.Precision.HIGHEST
    )
    scaled = (rotated.reshape(train_rows, local_layers, feat_size) / eig_values[None]).astype(
        jnp.bfloat16
    )
    scaled_flat = scaled.reshape(train_rows, local_layers * feat_size)
    query_flat = queries.reshape(query_rows, local_layers * feat_size)
    layer_devices = lax.axis_size("layer")
    factor = 1.0 / jnp.sqrt(jnp.float32(local_layers * layer_devices * feat_size))
    partial_sum = lax.dot_general(
        lax.all_gather(scaled_flat, "query", axis=0, tiled=True),
        query_flat,
        (((1,), (1,)), ((), ())),
        preferred_element_type=jnp.float32,
    )
    ordered = partial_sum[train_order] * factor
    return lax.psum_scatter(ordered, "layer", scatter_dimension=0, tiled=True)


def solution(mesh):
    placed = (
        P("query", "layer", None),
        P("query", "layer", None),
        P("layer", None, None),
        P("layer", None, None),
        P("layer", None),
        P(),
    )
    return jax.shard_map(
        per_device, mesh=mesh, in_specs=placed, out_specs=P("layer", "query"), check_vma=False
    )
```

profile of v0, /device:TPU:16, one launch (start us, length us, event | category | flops | bytes accessed | tf_op | source)
XLA Modules:
  0.0 253.4 jit_solution(12795032566997530325)
XLA Ops:
  6.5 0.0 copy-start
  6.5 0.0 copy-start.1
  6.5 0.0 all-gather.2.cloned.1.call-start
  6.5 2.1 reshape.35
  8.6 0.0 copy-done
  8.6 1.0 fusion.4
  9.7 0.0 copy-done.1
  9.7 0.0 copy-start.2
  9.7 0.0 copy-start.3
  9.7 1.8 fusion.2
  11.6 0.7 transpose.5
  12.2 0.0 copy-done.2
  12.2 0.9 divide_convert_fusion
  13.1 0.0 all-gather.2.cloned.1.call-update
  13.2 0.0 reduce-scatter.2.cloned.1.call-start
  13.2 0.0 copy-done.3
  13.2 136.2 %all-gather.2.cloned.1.call-done = bf16[1024,4096]{1,0:T(8,128)(2,1)} async-done(((bf16[64,4096]{1,0:T(8,128)(2,1)}), bf16[1024,4096]{1,0:T(8,128)(2,1)}) %all-gather.2.cloned.1.call-update) | async-done | bytes 8388624 | tf_op jit(solution)/shard_map/all_gather | solution.py:23
  149.4 15.1 %fusion = f32[1024,1024]{1,0:T(8,128)} fusion(bf16[1024,4096]{1,0:T(8,128)(2,1)} %all-gather.2.cloned.1.call-done, bf16[1024,1,4096]{2,0,1:T(8,128)(2,1)} %param.6), kind=kOutput, calls=%fused_computation.1 | convolution fusion | flops 8589934592 | bytes 20971520 | tf_op jit(solution)/shard_map/dot_general | solution.py:22
  164.5 8.5 %gather_fusion = f32[1024,1024]{1,0:T(8,128)} fusion(f32[1024,1024]{1,0:T(8,128)} %fusion, s32[1024]{0:T(1024)S(1)} %fusion.6), kind=kCustom, calls=%fused_computation | custom fusion | bytes 8392704 | tf_op jit(solution)/shard_map/gather | solution.py:28
  173.1 5.0 %broadcast_multiply_fusion = f32[1024,1024]{1,0:T(8,128)} fusion(f32[1024,1024]{1,0:T(8,128)} %gather_fusion), kind=kLoop, calls=%fused_computation.3 | loop fusion | flops 1048576 | bytes 8388608 | tf_op jit(solution)/shard_map/mul | solution.py:28
  178.0 0.0 reduce-scatter.2.cloned.1.call-update
  178.0 68.5 %reduce-scatter.2.cloned.1.call-done = f32[64,1024]{1,0:T(8,128)} async-done(((f32[1024,1024]{1,0:T(8,128)}), f32[64,1024]{1,0:T(8,128)}) %reduce-scatter.2.cloned.1.call-update) | async-done | bytes 262160 | tf_op jit(solution)/shard_map/reduce_scatter | solution.py:29
  (1 shorter events, 0.0 us)
Async XLA Ops:
  6.5 2.1 copy-start
  6.5 3.1 %copy-start.1 = (f32[1,64,64]{2,1,0:T(8,128)S(1)}, f32[1,64,64]{2,1,0:T(8,128)}, u32[]{:S(2)}) copy-start(f32[1,64,64]{2,1,0:T(8,128)} %param.9) | copy-start | bytes 49156
  6.5 142.9 %all-gather.2.cloned.1.call-start = ((), (), s32[]{:S(2)}) async-start(), calls=%async_computation.1 | async-start | bytes 8912896 | tf_op jit(solution)/shard_map/all_gather | solution.py:23
  9.7 2.5 copy-start.2
  9.7 3.5 %copy-start.3 = (s32[1024]{0:T(1024)S(1)}, s32[1024]{0:T(1024)}, u32[]{:S(2)}) copy-start(s32[1024]{0:T(1024)} %param.11) | copy-start | bytes 12292
  13.2 233.4 %reduce-scatter.2.cloned.1.call-start = ((), (), s32[]{:S(2)}) async-start(), calls=%async_computation.2 | async-start | bytes 4456448 | tf_op jit(solution)/shard_map/reduce_scatter | solution.py:29
Sparse Core Ops, SparseCore 0:
  13.3 136.1 all-gather.1
  178.2 68.3 reduce-scatter.1
where the time goes:
time: 254 us; the launch traced here: 253 us
  waiting for transfers between devices  205 us (81%)
  matrix products  17.9 us (7%)
  between operations  13.5 us (5%)
  local copies, waits for them, and re-layouts  11.3 us (4%)
  other arithmetic  5.89 us (2%)
    all_gather x1, waiting for transfers between devices, per_device(): lax.all_gather(scaled_flat, 'query', axis=0, tiled=True)  136 us
    reduce_scatter x1, waiting for transfers between devices, per_device(): return lax.psum_scatter(ordered, 'layer', scatter_dimension=0, tiled=True)  68.5 us
    dot_general x1, matrix products, per_device(): lax.dot_general(lax.all_gather(scaled_flat, 'query', axis=0, tiled=True),...  15.1 us
    gather x1, local copies, waits for them, and re-layouts, per_device(): ordered = partial_sum[train_order] * factor  8.54 us
  transfers between devices with their start and end apart: 2, of which 2 were waited for; matrix products, arithmetic and copies ran while one was open for 0% of the time, Pallas kernels for 0%

commit v1 on v0

--- a/solution.py
+++ b/solution.py
@@ -19,8 +19,17 @@
     query_flat = queries.reshape(query_rows, local_layers * feat_size)
     layer_devices = lax.axis_size("layer")
     factor = 1.0 / jnp.sqrt(jnp.float32(local_layers * layer_devices * feat_size))
+
+    def fill_the_columns(sample):
+        return jnp.concatenate(
+            lax.all_to_all(
+                jnp.stack(tuple((sample for _ in range(lax.axis_size("query"))))), "query", 0, 0
+            ),
+            axis=0,
+        )
+
     partial_sum = lax.dot_general(
-        lax.all_gather(scaled_flat, "query", axis=0, tiled=True),
+        fill_the_columns(scaled_flat),
         query_flat,
         (((1,), (1,)), ((), ())),
         preferred_element_type=jnp.float32,

time: 254 us -> 325 us (1.28)
  waiting for transfers between devices: 205 us -> 261 us
  starting transfers between devices: 0.04 us -> 11.6 us
  local copies, waits for them, and re-layouts: 11.3 us -> 15.6 us
    all_to_all x0 -> x1, waiting for transfers between devices: none -> 190 us  [fill_the_columns(): lax.all_to_all(jnp.stack(tuple((sample for _ in range(lax.axis_size('quer...]
    all_gather x1 -> x0, waiting for transfers between devices: 136 us -> none  [per_device(): lax.all_gather(scaled_flat, 'query', axis=0, tiled=True)]
    all_to_all x0 -> x1, starting transfers between devices: none -> 11.6 us  [fill_the_columns(): lax.all_to_all(jnp.stack(tuple((sample for _ in range(lax.axis_size('quer...]
    another operation x0 -> x1, local copies, waits for them, and re-layouts: none -> 4.28 us  [fill_the_columns(): jnp.stack(tuple((sample for _ in range(lax.axis_size('query')))))]
where the time goes in v1:
time: 325 us
  waiting for transfers between devices  261 us (80%)
  matrix products  17.9 us (6%)
  local copies, waits for them, and re-layouts  15.6 us (5%)
  between operations  13.5 us (4%)
  starting transfers between devices  11.6 us (4%)
  other arithmetic  5.06 us (2%)
    all_to_all x1, waiting for transfers between devices, fill_the_columns(): lax.all_to_all(jnp.stack(tuple((sample for _ in range(lax.axis_size('quer...  190 us
    reduce_scatter x1, waiting for transfers between devices, per_device(): return lax.psum_scatter(ordered, 'layer', scatter_dimension=0, tiled=True)  70.7 us
    dot_general x1, matrix products, per_device(): lax.dot_general(fill_the_columns(scaled_flat), query_flat, (((1,), (1,)),...  15.1 us
    all_to_all x1, starting transfers between devices, fill_the_columns(): lax.all_to_all(jnp.stack(tuple((sample for _ in range(lax.axis_size('quer...  11.6 us
    gather x1, local copies, waits for them, and re-layouts, per_device(): ordered = partial_sum[train_order] * factor  8.55 us
  transfers between devices with their start and end apart: 2, of which 2 were waited for; matrix products, arithmetic and copies ran while one was open for 0% of the time, Pallas kernels for 0%

profile of v1, /device:TPU:16, one launch (start us, length us, event | category | flops | bytes accessed | tf_op | source)
XLA Modules:
  0.0 324.6 jit_solution(16178320465056911024)
XLA Ops:
  6.5 0.0 copy-start
  6.5 0.0 copy-start.1
  6.5 2.1 reshape.40
  8.6 0.0 copy-done
  8.6 1.1 fusion.4
  9.7 0.0 copy-done.1
  9.7 0.0 copy-start.2
  9.7 1.8 fusion.2
  11.5 0.7 transpose.5
  12.1 0.0 copy-done.2
  12.2 0.1 divide_convert_fusion
  12.2 4.3 %stack.3 = bf16[16,64,4096]{2,1,0:T(8,128)(2,1)} broadcast(bf16[64,4096]{1,0:T(8,128)(2,1)S(1)} %divide_convert_fusion), dimensions={1,2} | broadcast | bytes 8912896 | tf_op jit(solution)/shard_map/stack | solution.py:26
  16.5 0.0 copy-start.3
  16.5 11.6 %all-to-all-start = ((bf16[16,64,4096]{2,1,0:T(8,128)(2,1)}), bf16[16,64,4096]{2,1,0:T(8,128)(2,1)}, u32[]{:S(2)}, u32[]{:S(2)}) async-start(bf16[16,64,4096]{2,1,0:T(8,128)(2,1)} %stack.3), calls=%async_computation | async-start | bytes 16777216 | tf_op jit(solution)/shard_map/all_to_all | solution.py:25
  28.1 0.0 reduce-scatter.2.cloned.1.call-start
  28.1 0.0 copy-done.3
  28.2 190.2 %all-to-all-done = bf16[16,64,4096]{2,1,0:T(8,128)(2,1)} async-done(((bf16[16,64,4096]{2,1,0:T(8,128)(2,1)}), bf16[16,64,4096]{2,1,0:T(8,128)(2,1)}, u32[]{:S(2)}, u32[]{:S(2)}) %all-to-all-start) | async-done | bytes 8388640 | tf_op jit(solution)/shard_map/all_to_all | solution.py:25
  218.4 15.1 %fusion = f32[1024,1024]{1,0:T(8,128)} fusion(bf16[1024,4096]{1,0:T(8,128)(2,1)} %bitcast.5, bf16[1024,1,4096]{2,0,1:T(8,128)(2,1)} %param.6), kind=kOutput, calls=%fused_computation.1 | convolution fusion | flops 8589934592 | bytes 20971520 | tf_op jit(solution)/shard_map/dot_general | solution.py:31
  233.5 8.6 %gather_fusion = f32[1024,1024]{1,0:T(8,128)} fusion(f32[1024,1024]{1,0:T(8,128)} %fusion, s32[1024]{0:T(1024)S(1)} %fusion.6), kind=kCustom, calls=%fused_computation | custom fusion | bytes 8392704 | tf_op jit(solution)/shard_map/gather | solution.py:37
  242.0 5.0 %broadcast_multiply_fusion = f32[1024,1024]{1,0:T(8,128)} fusion(f32[1024,1024]{1,0:T(8,128)} %gather_fusion), kind=kLoop, calls=%fused_computation.3 | loop fusion | flops 1048576 | bytes 8388608 | tf_op jit(solution)/shard_map/mul | solution.py:37
  247.0 0.0 reduce-scatter.2.cloned.1.call-update
  247.0 70.7 %reduce-scatter.2.cloned.1.call-done = f32[64,1024]{1,0:T(8,128)} async-done(((f32[1024,1024]{1,0:T(8,128)}), f32[64,1024]{1,0:T(8,128)}) %reduce-scatter.2.cloned.1.call-update) | async-done | bytes 262160 | tf_op jit(solution)/shard_map/reduce_scatter | solution.py:38
  (1 shorter events, 0.0 us)
Async XLA Ops:
  6.5 2.1 copy-start
  6.5 3.1 copy-start.1
  9.7 2.5 copy-start.2
  16.5 11.6 %copy-start.3 = (s32[1024]{0:T(1024)S(1)}, s32[1024]{0:T(1024)}, u32[]{:S(2)}) copy-start(s32[1024]{0:T(1024)} %param.11) | copy-start | bytes 12292
  16.5 201.8 %all-to-all-start = ((bf16[16,64,4096]{2,1,0:T(8,128)(2,1)}), bf16[16,64,4096]{2,1,0:T(8,128)(2,1)}, u32[]{:S(2)}, u32[]{:S(2)}) async-start(bf16[16,64,4096]{2,1,0:T(8,128)(2,1)} %stack.3), calls=%async_computation | async-start | bytes 16777216 | tf_op jit(solution)/shard_map/all_to_all | solution.py:25
  28.1 289.6 %reduce-scatter.2.cloned.1.call-start = ((), (), s32[]{:S(2)}) async-start(), calls=%async_computation.2 | async-start | bytes 4456448 | tf_op jit(solution)/shard_map/reduce_scatter | solution.py:38
Sparse Core Ops, SparseCore 0:
  247.1 70.5 reduce-scatter.1
